TPU v7x, 32 devices: a whole 2x2x4 slice. The times are simulated.
32 devices in a mesh: groups: 2 (over y), pool: 4 (over x, core), tp: 4 (over z).
Axes of the slice: x: 2, y: 2, z: 4, core: 2. Of those that a mesh axis runs over, the one named last changes fastest.
Arguments:
- queries: bfloat16 [8, 128, 16, 128], P(('groups', 'pool'), None, 'tp'), parts along dimension 0, may hold values from -8 to 8
- suffix_kv: bfloat16 [8, 128, 2, 256], P(('groups', 'pool')), parts along dimension 0, may hold values from -8 to 8
- kv_pool: bfloat16 [192, 2, 128, 256], P(('groups', 'pool', 'tp')), parts along dimension 0, may hold values from -6 to 6
- page_map: int32 [192], P('groups'), parts along dimension 0, may hold values from 0 to 95, as said below
- hit_pages: int32 [8, 16], P('groups'), parts along dimension 0, may hold values from 0 to 95, as said below
- suffix_lengths: int32 [8], P(('groups', 'pool')), parts along dimension 0, may hold values from 32 to 128, as said below
- out_weight: bfloat16 [2048, 8192], P('tp'), may hold values from -0.5 to 0.5
Outputs:
- layer_update: bfloat16 [8, 128, 8192], P(('groups', 'pool'), 'tp'), parts along dimension 0
There are 2 independent parts, one for each index of `groups`. A program takes and returns all parts, laid end to end along the dimension named above; an argument that names none is the same for every part. Nothing has to cross between parts.
Inputs may be any that keep to these rules, and one draw needn't show every extreme that they name: `page_map`: a permutation of the physical pages. `hit_pages`: the 16 logical pages of one session are different; through page_map at most 2 pages of one session lie on one device, and one device holds exactly 2 pages of every session. `suffix_lengths`: some session has all 128 suffix tokens live.
All inputs are finite; a program needn't handle non-finite values.
Results may differ from a plain program's by a relative error of at most 0.012.
Values may be sent and summed in bfloat16 or wider, within the bound.
A program may use at most 128 MiB of HBM per device.

v0:
```python
import math

import jax
import jax.numpy as jnp
from jax import lax
from jax.sharding import PartitionSpec as P

CAP = 2


NEG_FILL = -1e30


def sender_slots(owner_all, slot_local, self_owner):
    owned = owner_all == self_owner
    owned_rank = jnp.cumsum(owned.astype(jnp.int32), axis=1) - 1
    columns = []
    for slot_index in range(CAP):
        taken = jnp.logical_and(owned, owned_rank == slot_index)
        columns.append(jnp.sum(jnp.where(taken, slot_local, 0), axis=1))
    return jnp.stack(columns, axis=1)


def per_device(queries, suffix_kv, kv_pool, page_map, hit_pages, suffix_lengths, out_weight):
    sessions = lax.axis_size("pool")
    tp_count = lax.axis_size("tp")
    tp_rank = lax.axis_index("tp")
    pool_rank = lax.axis_index("pool")
    owners = sessions * tp_count
    pages_dev = kv_pool.shape[0]
    kv_heads = kv_pool.shape[1]
    page_len = kv_pool.shape[2]
    head_dim = kv_pool.shape[3] // 2
    physical = jnp.take(page_map, hit_pages, axis=0)
    owner_all = physical // pages_dev
    slot_local = physical % pages_dev
    self_owner = pool_rank * tp_count + tp_rank
    chosen = sender_slots(owner_all, slot_local, self_owner)
    tp_ids = jnp.arange(tp_count, dtype=jnp.int32)
    page_index = jnp.broadcast_to(chosen[:, None, :], (sessions, tp_count, CAP))
    slot_width = page_index.shape[2]
    flat_index = page_index * kv_heads + (tp_ids // 2)[None, :, None]
    pool_rows = kv_pool.reshape(pages_dev * kv_heads, page_len, 2 * head_dim)
    outgoing = jnp.take(pool_rows, flat_index.reshape(-1), axis=0)
    outgoing = outgoing.reshape(sessions, tp_count, slot_width, page_len, 2 * head_dim)
    arrived = lax.all_to_all(
        outgoing.reshape(owners, slot_width, page_len, 2 * head_dim),
        ("pool", "tp"),
        split_axis=0,
        concat_axis=0,
        tiled=True,
    )
    own_owners = lax.dynamic_index_in_dim(owner_all, pool_rank, 0, keepdims=False)
    owner_ids = jnp.arange(owners, dtype=jnp.int32)
    page_counts = jnp.sum((own_owners[:, None] == owner_ids[None, :]).astype(jnp.int32), axis=0)
    slot_valid = jnp.arange(CAP, dtype=jnp.int32)[None, :] < page_counts[:, None]
    inv_root = 1.0 / math.sqrt(head_dim)
    kv_head = tp_rank // 2
    query_heads = jnp.transpose(queries[0], (1, 0, 2))
    suffix_len = queries.shape[1]
    own_suffix = lax.dynamic_index_in_dim(suffix_kv[0], kv_head, 1, keepdims=False)
    positions = jnp.arange(suffix_len, dtype=jnp.int32)
    causal = positions[None, :] <= positions[:, None]
    scores = (
        jnp.einsum(
            "hqd,kd->hqk", query_heads, own_suffix[:, :head_dim], preferred_element_type=jnp.float32
        )
        * inv_root
    )
    scores = jnp.where(causal[None], scores, NEG_FILL)
    running_peak = jnp.max(scores, axis=2)
    weights = jnp.where(causal[None], jnp.exp(scores - running_peak[..., None]), 0.0)
    running_total = jnp.sum(weights, axis=2)
    running_acc = jnp.einsum(
        "hqk,kd->hqd",
        weights.astype(jnp.bfloat16),
        own_suffix[:, head_dim:],
        preferred_element_type=jnp.float32,
    )
    slots_all = owners * CAP
    block_slots = min(32, slots_all)
    block_count = slots_all // block_slots
    key_blocks = arrived.reshape(block_count, block_slots * page_len, 2 * head_dim)
    mask_blocks = jnp.repeat(slot_valid.reshape(block_count, block_slots), page_len, axis=1)

    def visit_block(state, block_data):
        peak_now, total_now, acc_now = state
        block_keys, block_mask = block_data
        block_scores = (
            jnp.einsum(
                "hqd,kd->hqk",
                query_heads,
                block_keys[:, :head_dim],
                preferred_element_type=jnp.float32,
            )
            * inv_root
        )
        block_peak = jnp.max(jnp.where(block_mask[None, None, :], block_scores, NEG_FILL), axis=2)
        new_peak = jnp.maximum(peak_now, block_peak)
        factor = jnp.exp(peak_now - new_peak)
        block_weights = jnp.where(
            block_mask[None, None, :], jnp.exp(block_scores - new_peak[..., None]), 0.0
        )
        new_total = total_now * factor + jnp.sum(block_weights, axis=2)
        new_acc = acc_now * factor[..., None] + jnp.einsum(
            "hqk,kd->hqd",
            block_weights.astype(jnp.bfloat16),
            block_keys[:, head_dim:],
            preferred_element_type=jnp.float32,
        )
        return ((new_peak, new_total, new_acc), None)

    final_state, unused = lax.scan(
        visit_block, (running_peak, running_total, running_acc), (key_blocks, mask_blocks)
    )
    final_peak, final_total, final_acc = final_state
    attended = (final_acc / final_total[..., None]).astype(jnp.bfloat16)
    flat_rows = jnp.transpose(attended, (1, 0, 2)).reshape(suffix_len, -1)
    live_rows = positions < suffix_lengths[0]
    flat_rows = jnp.where(live_rows[:, None], flat_rows, jnp.zeros_like(flat_rows))
    rows_dev = suffix_len // tp_count
    summed = lax.psum_scatter(
        jnp.dot(flat_rows, out_weight, preferred_element_type=jnp.float32).astype(jnp.bfloat16),
        "tp",
        scatter_dimension=0,
        tiled=True,
    ).astype(jnp.float32)
    return summed.astype(jnp.bfloat16).reshape(1, rows_dev, summed.shape[1])


def solution(mesh):
    in_specs = (
        P(("groups", "pool"), None, "tp", None),
        P(("groups", "pool"), None, None, None),
        P(("groups", "pool", "tp"), None, None, None),
        P("groups"),
        P("groups", None),
        P(("groups", "pool")),
        P("tp", None),
    )
    out_specs = P(("groups", "pool"), "tp", None)
    return jax.shard_map(
        per_device, mesh=mesh, in_specs=in_specs, out_specs=out_specs, check_vma=False
    )
```

profile of v0, /device:TPU:0, one launch (start us, length us, event | category | flops | bytes accessed | tf_op | source)
XLA Modules:
  0.0 129.0 jit_solution(5844470075494681356)
XLA Ops:
  6.5 0.0 copy-start
  6.5 0.0 copy-start.2
  6.5 0.0 copy-start.1
  6.6 0.8 compare_select_fusion
  7.3 0.1 reshape.134
  7.4 1.4 %gather_fusion = s32[64]{0:T(128)S(1)} fusion(s32[96]{0:T(128)} %param.10, s32[1024]{0:T(1024)S(1)} %pad_clamp_fusion.1), kind=kCustom, calls=%fused_computation | custom fusion | bytes 768 | tf_op jit(solution)/shard_map/jit(_take)/gather | solution.py:34
  8.8 0.1 reshape.133
  8.9 0.7 fusion.25
  9.6 0.2 reduce_window_sum.11
  9.8 0.8 select_reduce_fusion.2
  10.7 0.1 copy.31
  10.8 0.1 broadcast_add_fusion
  10.9 0.1 add.117
  11.0 0.1 copy.40
  11.1 0.1 add.110
  11.2 0.1 copy.33
  11.3 0.0 copy-done
  11.3 0.7 gather_fusion.1
  12.0 1.6 %broadcast_select_fusion = bf16[16,2,128,256]{3,2,1,0:T(8,128)(2,1)} fusion(bf16[16,2,128,256]{3,2,1,0:T(8,128)(2,1)S(1)} %bitcast.80, pred[16,2]{1,0:T(8,128)(4,1)S(1)} %copy.33), kind=kLoop, calls=%fused_computation.9 | loop fusion | flops 1048576 | bytes 4194336 | tf_op jit(solution)/shard_map/jit(_take)/select_n | solution.py:44
  13.6 7.4 %all-to-all-start = ((bf16[16,2,128,256]{3,2,1,0:T(8,128)(2,1)}), bf16[16,2,128,256]{3,2,1,0:T(8,128)(2,1)S(1)}, u32[]{:S(2)}, u32[]{:S(2)}) async-start(bf16[16,2,128,256]{3,2,1,0:T(8,128)(2,1)} %broadcast_select_fusion), calls=%async_computation | async-start | bytes 4194304 | tf_op jit(solution)/shard_map/all_to_all | solution.py:46
  20.9 0.0 reduce-scatter.2.cloned.1.call-start
  21.0 0.1 convert_reduce_fusion
  21.1 0.1 iota_compare_fusion.2
  21.2 0.1 lt.82
  21.3 0.0 copy-done.2
  21.3 0.1 constant_dynamic-slice_fusion
  22.2 0.0 copy-done.1
  22.2 0.2 fusion.26
  22.4 0.1 fusion.10
  22.4 0.1 broadcast_bitcast_fusion
  22.5 47.9 %all-to-all-done = bf16[16,2,128,256]{3,2,1,0:T(8,128)(2,1)S(1)} async-done(((bf16[16,2,128,256]{3,2,1,0:T(8,128)(2,1)}), bf16[16,2,128,256]{3,2,1,0:T(8,128)(2,1)S(1)}, u32[]{:S(2)}, u32[]{:S(2)}) %all-to-all-start) | async-done | bytes 2097184 | tf_op jit(solution)/shard_map/all_to_all | solution.py:46
  70.4 0.0 slice-start
  70.4 1.3 %select_reduce_fusion = (f32[4,128]{1,0:T(4,128)S(1)}, f32[4096,4,128]{2,0,1:T(8,128)S(1)}) fusion(pred[4096]{0:T(1024)(128)(4,1)S(1)} %broadcast_bitcast_fusion, bf16[4,128,128]{2,0,1:T(4,128)(2,1)S(1)} %bitcast.86, bf16[4096,256]{1,0:T(8,128)(2,1)S(1)} %bitcast.81), kind=kOutput, calls=%fused_computation.6 | convolution fusion | flops 543161856 | bytes 9574400 | tf_op jit(solution)/shard_map/while/body/eval_jaxpr/hqd,kd->hqk/dot_general | solution.py:90
  71.7 0.0 slice-start.1
  71.7 2.0 %fusion.7 = f32[128,4,128]{0,2,1:T(8,128)S(1)} fusion(f32[4096,4,128]{2,0,1:T(8,128)S(1)} %get-tuple-element.36, f32[4,128]{1,0:T(4,128)S(1)} %max.19, pred[4096]{0:T(1024)(128)(4,1)S(1)} %broadcast_bitcast_fusion, bf16[4096,256]{1,0:T(8,128)(2,1)S(1)} %bitcast.82), kind=kOutput, calls=%fused_computation.17 | convolution fusion | flops 545259520 | bytes 9705472 | tf_op jit(solution)/shard_map/while/body/eval_jaxpr/hqk,kd->hqd/dot_general | solution.py:105
  73.7 2.7 %bitcast_reduce_fusion = f32[4,128]{1,0:T(4,128)S(1)} fusion(f32[4096,4,128]{2,0,1:T(8,128)S(1)} %get-tuple-element.36, f32[4,128]{1,0:T(4,128)S(1)} %max.19, pred[4096]{0:T(1024)(128)(4,1)S(1)} %broadcast_bitcast_fusion), kind=kLoop, calls=%fused_computation.3 | loop fusion | flops 8388096 | bytes 8396800 | tf_op jit(solution)/shard_map/while/body/eval_jaxpr/reduce_sum | solution.py:104
  76.4 0.2 fusion.8
  76.7 0.0 slice-done
  76.7 0.0 slice-done.1
  76.7 2.7 %convolution_convert_fusion = bf16[128,8192]{1,0:T(8,128)(2,1)} fusion(bf16[128,512]{0,1:T(8,128)(2,1)S(1)} %bitcast_select_fusion, bf16[512,8192]{1,0:T(8,128)(2,1)S(1)} %bitcast.79), kind=kOutput, calls=%fused_computation.2 | convolution fusion | flops 1074790400 | bytes 10616832 | tf_op jit(solution)/shard_map/dot_general | solution.py:123
  79.4 0.0 reduce-scatter.2.cloned.1.call-update
  79.5 42.7 %reduce-scatter.2.cloned.1.call-done = bf16[32,8192]{1,0:T(8,128)(2,1)} async-done(((bf16[128,8192]{1,0:T(8,128)(2,1)}), bf16[32,8192]{1,0:T(8,128)(2,1)}) %reduce-scatter.2.cloned.1.call-update) | async-done | bytes 524304 | tf_op jit(solution)/shard_map/reduce_scatter | solution.py:122
  (16 shorter events, 0.1 us)
Async XLA Ops:
  6.5 4.7 %copy-start = (bf16[6,2,128,256]{3,2,1,0:T(8,128)(2,1)S(1)}, bf16[6,2,128,256]{3,2,1,0:T(8,128)(2,1)}, u32[]{:S(2)}) copy-start(bf16[6,2,128,256]{3,2,1,0:T(8,128)(2,1)} %param.9) | copy-start | bytes 2359300
  6.5 14.8 %copy-start.2 = (bf16[1,128,2,256]{3,2,1,0:T(2,128)(2,1)S(1)}, bf16[1,128,2,256]{3,2,1,0:T(2,128)(2,1)}, u32[]{:S(2)}) copy-start(bf16[1,128,2,256]{3,2,1,0:T(2,128)(2,1)} %param.8) | copy-start | bytes 393220
  6.5 15.6 %copy-start.1 = (bf16[1,128,4,128]{3,2,1,0:T(4,128)(2,1)S(1)}, bf16[1,128,4,128]{3,2,1,0:T(4,128)(2,1)}, u32[]{:S(2)}) copy-start(bf16[1,128,4,128]{3,2,1,0:T(4,128)(2,1)} %param.7) | copy-start | bytes 393220
  13.6 56.8 %all-to-all-start = ((bf16[16,2,128,256]{3,2,1,0:T(8,128)(2,1)}), bf16[16,2,128,256]{3,2,1,0:T(8,128)(2,1)S(1)}, u32[]{:S(2)}, u32[]{:S(2)}) async-start(bf16[16,2,128,256]{3,2,1,0:T(8,128)(2,1)} %broadcast_select_fusion), calls=%async_computation | async-start | bytes 4194304 | tf_op jit(solution)/shard_map/all_to_all | solution.py:46
  20.9 101.2 %reduce-scatter.2.cloned.1.call-start = ((), (), s32[]{:S(2)}) async-start(), calls=%async_computation.2 | async-start | bytes 2621440 | tf_op jit(solution)/shard_map/reduce_scatter | solution.py:122
  70.4 6.3 %slice-start = ((s8[8388608]{0:T(1024)(128)(4,1)}), s8[4194304]{0:T(1024)(128)(4,1)S(1)}, s32[]{:S(2)}) async-start(s8[8388608]{0:T(1024)(128)(4,1)} %bitcast.78), calls=%async_computation.3 | async-start | bytes 8388608
  71.7 5.0 %slice-start.1 = ((s8[8388608]{0:T(1024)(128)(4,1)}), s8[4194304]{0:T(1024)(128)(4,1)S(1)}, s32[]{:S(2)}) async-start(s8[8388608]{0:T(1024)(128)(4,1)} %bitcast.78), calls=%async_computation.4 | async-start | bytes 8388608
Sparse Core Ops, SparseCore 0:
  79.6 42.5 reduce-scatter.1
where the time goes:
time: 129 us
  waiting for transfers between devices  90.6 us (70%)
  between operations  14.3 us (11%)
  starting transfers between devices  7.4 us (6%)
  other arithmetic  7.24 us (6%)
  matrix products  6.42 us (5%)
  local copies, waits for them, and re-layouts  3.1 us (2%)
    all_to_all x1, waiting for transfers between devices, per_device(): lax.all_to_all(outgoing.reshape(owners, slot_width, page_len, 2 * head_di...  47.9 us
    reduce_scatter x1, waiting for transfers between devices, per_device(): lax.psum_scatter(jnp.dot(flat_rows, out_weight, preferred_element_type=jn...  42.7 us
    all_to_all x1, starting transfers between devices, per_device(): lax.all_to_all(outgoing.reshape(owners, slot_width, page_len, 2 * head_di...  7.36 us
    dot_general x1, matrix products, per_device(): jnp.dot(flat_rows, out_weight, preferred_element_type=jnp.float32)  2.73 us
    reduce_sum x1, other arithmetic, visit_block(): new_total = total_now * factor + jnp.sum(block_weights, axis=2)  2.71 us
  transfers between devices with their start and end apart: 2, of which 2 were waited for; matrix products, arithmetic and copies ran while one was open for 1% of the time, Pallas kernels for 0%

commit v1 on v0

v1 whole, which is shorter than its diff:
```python
import functools
import math

import jax
import jax.numpy as jnp
from jax import lax
from jax.experimental import pallas as pl
from jax.experimental.pallas import tpu as pltpu
from jax.sharding import PartitionSpec as P

CAP = 2
STAT = 8
LANES = 128
NEG_FILL = -1e30
MESH = pl.DeviceIdType.MESH
F32 = jnp.float32
BF16 = jnp.bfloat16


def kernel(
    pools, tps, block,
    map_ref, hit_ref, len_ref, q_ref, suf_ref, pool_ref, w_hbm,
    out_ref,
    w_ref, kv, kv_send, q_all, o_send, o_recv, s_send, s_recv, o_suf, attn, part, own, c_send, c_up, c_dn,
    w_sem, kv_ss, kv_rs, q_ss, q_rs, o_ss, o_rs, s_ss, s_rs, c_ss, up_rs, dn_rs,
):
    me_p, me = lax.axis_index("pool"), lax.axis_index("tp")
    pages_dev, kv_heads, page, width = pool_ref.shape
    hd = width // 2
    heads, rows, _ = q_ref.shape
    hits = hit_ref.shape[1]
    group = heads * tps // kv_heads
    blocks = own.shape[0]
    rows_dev = rows // tps
    scale = math.log2(math.e) / math.sqrt(hd)

    w_copy = pltpu.make_async_copy(w_hbm, w_ref, w_sem)
    w_copy.start()

    barrier = pltpu.get_barrier_semaphore()
    for d in range(1, pools):
        pl.semaphore_signal(barrier, inc=1, device_id={"pool": lax.rem(me_p + d, pools)}, device_id_type=MESH)
    for d in range(1, tps):
        pl.semaphore_signal(barrier, inc=1, device_id={"tp": lax.rem(me + d, tps)}, device_id_type=MESH)
    pl.semaphore_wait(barrier, pools + tps - 2)

    def q_copy(d):
        return pltpu.make_async_remote_copy(
            src_ref=q_ref, dst_ref=q_all.at[d - 1], send_sem=q_ss.at[d - 1], recv_sem=q_rs.at[d - 1],
            device_id={"tp": lax.rem(me + d, tps)}, device_id_type=MESH,
        )

    def kv_copy(d):
        return pltpu.make_async_remote_copy(
            src_ref=kv_send.at[d - 1], dst_ref=kv.at[d], send_sem=kv_ss.at[d - 1], recv_sem=kv_rs.at[d - 1],
            device_id={"pool": lax.rem(me_p + d, pools)}, device_id_type=MESH,
        )

    base = (me_p * tps + me) * pages_dev

    def choose(session):
        def body(i, carry):
            first, second, rank = carry
            local = map_ref[hit_ref[session, i]] - base
            owned = jnp.logical_and(local >= 0, local < pages_dev)
            first = jnp.where(jnp.logical_and(owned, rank == 0), local, first)
            second = jnp.where(jnp.logical_and(owned, rank == 1), local, second)
            return first, second, rank + owned.astype(jnp.int32)

        zero = jnp.int32(0)
        return lax.fori_loop(0, hits, body, (zero, zero, zero), unroll=hits <= 16)[:2]

    order = sorted(range(1, pools), key=lambda d: -min(d, pools - d))
    for d in order:
        first, second = choose(lax.rem(me_p + d, pools))
        kv_send[d - 1, 0] = pool_ref[first]
        kv_send[d - 1, 1] = pool_ref[second]
        kv_copy(d).start()
    for d in range(1, tps):
        q_copy(d).start()
    first, second = choose(me_p)
    kv[0, 0] = pool_ref[first]
    kv[0, 1] = pool_ref[second]

    bases = [(lax.rem(me_p + pools - d, pools) * tps + me) * pages_dev for d in range(pools)]

    def count(i, carry):
        physical = map_ref[hit_ref[me_p, i]]
        return tuple(
            c + jnp.logical_and(physical >= b, physical < b + pages_dev).astype(jnp.int32)
            for c, b in zip(carry, bases)
        )

    counts = lax.fori_loop(0, hits, count, tuple(jnp.int32(0) for _ in bases), unroll=hits <= 16)
    lane2 = lax.broadcasted_iota(jnp.int32, (1, CAP * page), 1)
    biases = [
        jnp.where(lane2 < page, jnp.where(c > 0, 0.0, NEG_FILL), jnp.where(c > 1, 0.0, NEG_FILL)).astype(F32)
        for c in counts
    ]

    def softmax(scores, values):
        top = functools.reduce(jnp.maximum, scores)
        peak = jnp.max(top, axis=1, keepdims=True) * scale
        weights = [jnp.exp2(s * scale - peak) for s in scores]
        total = jnp.sum(functools.reduce(jnp.add, weights), axis=1, keepdims=True)
        acc = functools.reduce(
            jnp.add,
            [jnp.dot(x.astype(BF16), v, preferred_element_type=F32) for x, v in zip(weights, values)],
        )
        return acc / total, peak + jnp.log2(total)

    def dot_t(a, b):
        return lax.dot_general(a, b, (((1,), (1,)), ((), ())), preferred_element_type=F32)

    q_own = q_ref[...].reshape(heads * rows, hd)
    scores = dot_t(q_own, suf_ref[:, :hd])
    row = lax.broadcasted_iota(jnp.int32, (heads, rows, rows), 1).reshape(heads * rows, rows)
    column = lax.broadcasted_iota(jnp.int32, (heads * rows, rows), 1)
    scores = jnp.where(column <= row, scores, NEG_FILL)
    att_suf, lse_suf = softmax([scores], [suf_ref[:, hd:]])
    o_suf[...] = att_suf

    def prefix(q, rank):
        g = lax.div(rank * heads, group)
        keys, values = [], []
        for d in range(pools):
            both = kv[d, :, g].reshape(CAP * page, width)
            keys.append(both[:, :hd])
            values.append(both[:, hd:])
        return softmax([dot_t(q, k) + b for k, b in zip(keys, biases)], values)

    for d in range(1, pools):
        kv_copy(d).wait_recv()
    for d in range(s_recv.shape[0]):
        if d >= tps - 1:
            s_recv[d] = jnp.zeros_like(s_recv[d])

    def o_copy(d):
        return pltpu.make_async_remote_copy(
            src_ref=o_send.at[d - 1], dst_ref=o_recv.at[d - 1], send_sem=o_ss.at[d - 1], recv_sem=o_rs.at[d - 1],
            device_id={"tp": lax.rem(me + d, tps)}, device_id_type=MESH,
        )

    def s_copy(d):
        return pltpu.make_async_remote_copy(
            src_ref=s_send.at[d - 1], dst_ref=s_recv.at[d - 1], send_sem=s_ss.at[d - 1], recv_sem=s_rs.at[d - 1],
            device_id={"tp": lax.rem(me + d, tps)}, device_id_type=MESH,
        )

    lane = lax.broadcasted_iota(jnp.int32, (rows, LANES), 1)

    @pl.loop(1, tps)
    def _(d):
        q_copy(tps - d).wait_recv()
        att, lse = prefix(q_all[tps - d - 1].reshape(heads * rows, hd), lax.rem(me + d, tps))
        o_send[d - 1] = att.astype(BF16).reshape(heads, rows, hd)
        o_copy(d).start()
        tile = jnp.zeros((rows, LANES), F32)
        for j in range(heads):
            tile = jnp.where(lane == j, lse[j * rows:(j + 1) * rows], tile)
        s_send[d - 1] = tile.T[:STAT]
        s_copy(d).start()

    att_own, lse_own = prefix(q_own, me)

    for d in range(1, tps):
        o_copy(d).wait_recv()
        s_copy(d).wait_recv()
    stats = s_recv[...].reshape(LANES, rows).T
    live = lax.broadcasted_iota(jnp.int32, (rows, 1), 0) < len_ref[0]
    for j in range(heads):
        here = slice(j * rows, (j + 1) * rows)
        logs = [lse_own[here], lse_suf[here]] + [
            stats[:, (d - 1) * STAT + j:(d - 1) * STAT + j + 1] for d in range(1, tps)
        ]
        parts = [att_own[here], o_suf[here]] + [o_recv[d - 1, j].astype(F32) for d in range(1, tps)]
        peak = functools.reduce(jnp.maximum, logs)
        shares = [jnp.exp2(x - peak) for x in logs]
        total = functools.reduce(jnp.add, shares)
        mixed = functools.reduce(jnp.add, [s * o for s, o in zip(shares, parts)]) / total
        attn[:, j * hd:(j + 1) * hd] = jnp.where(live, mixed, 0.0).astype(BF16)

    w_copy.wait()

    def c_copy(t, b, up):
        landing, sem, to = (c_up, up_rs, me + 1) if up else (c_dn, dn_rs, me + tps - 1)
        return pltpu.make_async_remote_copy(
            src_ref=c_send.at[t, b], dst_ref=landing.at[t, b], send_sem=c_ss.at[t, b], recv_sem=sem.at[t, b],
            device_id={"tp": lax.rem(to, tps)}, device_id_type=MESH,
        )

    def pass_on(t, b, up):
        first_one = me == 0 if up else me == tps - 1

        @pl.when(first_one)
        def _():
            c_send[t, b] = part[t].astype(BF16)

        @pl.when(jnp.logical_not(first_one))
        def _():
            c_copy(t, b, up).wait_recv()
            landing = c_up if up else c_dn
            c_send[t, b] = (part[t] + landing[t, b].astype(F32)).astype(BF16)

        c_copy(t, b, up).start()

    @pl.loop(0, blocks)
    def _(b):
        columns = pl.ds(pl.multiple_of(b * block, block), block)
        product = jnp.dot(attn[...], w_ref[:, columns], preferred_element_type=F32)
        for t in range(tps):
            part[t] = product[t * rows_dev:(t + 1) * rows_dev]
        own[b] = part[me]
        for far in range(tps - 1, 0, -1):
            @pl.when(me + far < tps)
            def _():
                pass_on(me + far, b, True)

            @pl.when(me >= far)
            def _():
                pass_on(me - far, b, False)

    @pl.loop(0, blocks)
    def _(b):
        @pl.when(me > 0)
        def _():
            c_copy(me, b, True).wait_recv()
            own[b] = own[b] + c_up[me, b].astype(F32)

        @pl.when(me < tps - 1)
        def _():
            c_copy(me, b, False).wait_recv()
            own[b] = own[b] + c_dn[me, b].astype(F32)

        out_ref[:, pl.ds(pl.multiple_of(b * block, block), block)] = own[b].astype(BF16)

    for d in range(1, pools):
        kv_copy(d).wait_send()
    for d in range(1, tps):
        q_copy(d).wait_send()
        o_copy(d).wait_send()
        s_copy(d).wait_send()

    @pl.loop(0, blocks)
    def _(b):
        for far in range(1, tps):
            @pl.when(me + far < tps)
            def _():
                c_copy(me + far, b, True).wait_send()

            @pl.when(me >= far)
            def _():
                c_copy(me - far, b, False).wait_send()


def per_device(pools, tps, queries, suffix_kv, kv_pool, page_map, hit_pages, suffix_lengths, out_weight):
    pages_dev, kv_heads, page, width = kv_pool.shape
    hd = width // 2
    rows, heads = queries.shape[1], queries.shape[2]
    model = out_weight.shape[1]
    block = min(1024, model)
    blocks = model // block
    rows_dev = rows // tps
    group = heads * tps // kv_heads
    q = jnp.transpose(queries[0], (1, 0, 2))
    suffix = lax.dynamic_index_in_dim(
        suffix_kv[0], lax.axis_index("tp") * heads // group, 1, keepdims=False
    )
    vmem = pl.BlockSpec(memory_space=pltpu.VMEM)
    smem = pl.BlockSpec(memory_space=pltpu.SMEM)
    dma = pltpu.SemaphoreType.DMA
    chain = (tps, blocks, rows_dev, block)
    out = pl.pallas_call(
        functools.partial(kernel, pools, tps, block),
        out_shape=jax.ShapeDtypeStruct((rows_dev, model), BF16),
        in_specs=[smem, smem, smem, vmem, vmem, vmem, pl.BlockSpec(memory_space=pl.ANY)],
        out_specs=vmem,
        scratch_shapes=[
            pltpu.VMEM(out_weight.shape, BF16),
            pltpu.VMEM((pools, CAP, kv_heads, page, width), BF16),
            pltpu.VMEM((pools - 1, CAP, kv_heads, page, width), BF16),
            pltpu.VMEM((tps - 1, heads, rows, hd), BF16),
            pltpu.VMEM((tps - 1, heads, rows, hd), BF16),
            pltpu.VMEM((tps - 1, heads, rows, hd), BF16),
            pltpu.VMEM((tps - 1, STAT, rows), F32),
            pltpu.VMEM((LANES // STAT, STAT, rows), F32),
            pltpu.VMEM((heads * rows, hd), F32),
            pltpu.VMEM((rows, heads * hd), BF16),
            pltpu.VMEM((tps, rows_dev, block), F32),
            pltpu.VMEM((blocks, rows_dev, block), F32),
            pltpu.VMEM(chain, BF16),
            pltpu.VMEM(chain, BF16),
            pltpu.VMEM(chain, BF16),
            dma,
            dma((pools - 1,)), dma((pools - 1,)),
            dma((tps - 1,)), dma((tps - 1,)),
            dma((tps - 1,)), dma((tps - 1,)),
            dma((tps - 1,)), dma((tps - 1,)),
            dma((tps, blocks)), dma((tps, blocks)), dma((tps, blocks)),
        ],
        compiler_params=pltpu.CompilerParams(
            collective_id=0, has_side_effects=True, vmem_limit_bytes=56 * 1024 * 1024
        ),
        cost_estimate=pl.CostEstimate(flops=3 * 10**9, bytes_accessed=12 * 10**6, transcendentals=2 * 10**6),
    )(page_map, hit_pages, suffix_lengths, q, suffix, kv_pool, out_weight)
    return out[None]


def solution(mesh):
    in_specs = (
        P(("groups", "pool"), None, "tp", None),
        P(("groups", "pool"), None, None, None),
        P(("groups", "pool", "tp"), None, None, None),
        P("groups"),
        P("groups", None),
        P(("groups", "pool")),
        P("tp", None),
    )
    out_specs = P(("groups", "pool"), "tp", None)
    return jax.shard_map(
        functools.partial(per_device, mesh.shape["pool"], mesh.shape["tp"]),
        mesh=mesh, in_specs=in_specs, out_specs=out_specs, check_vma=False,
    )
```

time: 129 us -> 83.5 us (0.65)
  waiting for transfers between devices: 90.6 us -> 0 us
  Pallas kernels: 0 us -> 78.1 us
  between operations: 14.3 us -> 0.7 us
  starting transfers between devices: 7.4 us -> 0 us
  other arithmetic: 7.24 us -> 0 us
  matrix products: 6.42 us -> 0 us
  local copies, waits for them, and re-layouts: 3.1 us -> 4.47 us
    pallas_call x0 -> x1, Pallas kernels: none -> 78.1 us  [per_device(): pl.pallas_call(functools.partial(kernel, pools, tps, block), out_shape=ja...]
    all_to_all x1 -> x0, waiting for transfers between devices: 47.9 us -> none  [per_device(): lax.all_to_all(outgoing.reshape(owners, slot_width, page_len, 2 * head_di...]
    reduce_scatter x1 -> x0, waiting for transfers between devices: 42.7 us -> none  [per_device(): lax.psum_scatter(jnp.dot(flat_rows, out_weight, preferred_element_type=jn...]
    all_to_all x1 -> x0, starting transfers between devices: 7.36 us -> none  [per_device(): lax.all_to_all(outgoing.reshape(owners, slot_width, page_len, 2 * head_di...]
    dot_general x5 -> x0, matrix products: 6.42 us -> none  [the longest x1 2.73 us: per_device(): jnp.dot(flat_rows, out_weight, preferred_element_type=jnp.float32)]
    unnamed x11 -> x5, local copies, waits for them, and re-layouts: 0.03 us -> 4.33 us
    reduce_sum x4 -> x0, other arithmetic: 3.71 us -> none  [the longest x1 2.71 us: visit_block(): new_total = total_now * factor + jnp.sum(block_weights, axis=2)]
    select_n x5 -> x0, other arithmetic: 2.41 us -> none  [the longest x2 1.61 us: per_device(): outgoing = jnp.take(pool_rows, flat_index.reshape(-1), axis=0)]
  transfers between devices with their start and end apart: 2 -> 0, of which waited for: 2 -> 0; matrix products, arithmetic and copies ran while one was open for 1% -> 0% of each run, Pallas kernels for 0% -> 0%
where the time goes in v1:
time: 83.5 us; the launch traced here: 83.2 us
  Pallas kernels  78.1 us (94%)
  local copies, waits for them, and re-layouts  4.47 us (5%)
    pallas_call x1, Pallas kernels, per_device(): pl.pallas_call(functools.partial(kernel, pools, tps, block), out_shape=ja...  78.1 us
    unnamed x5, local copies, waits for them, and re-layouts  4.33 us

profile of v1, /device:TPU:0, one launch (start us, length us, event | category | flops | bytes accessed | tf_op | source)
XLA Modules:
  0.0 83.2 jit_solution(6484626614713662540)
XLA Ops:
  0.0 0.0 copy-start
  0.7 0.2 copy-done
  0.9 0.1 constant_dynamic-slice_fusion
  1.1 0.6 copy.15
  1.7 1.6 %copy.14 = bf16[1,128,4,128]{3,1,2,0:T(8,128)(2,1)} copy(bf16[1,128,4,128]{3,2,1,0:T(4,128)(2,1)} %param.7) | data formatting | bytes 262144 | tf_op args[0]
  3.3 78.1 %shard_map.73 = bf16[32,8192]{1,0:T(8,128)(2,1)} custom-call(s32[96]{0:T(128)} %map_ref.1, s32[4,16]{1,0:T(4,128)} %hit_ref.1, s32[1]{0:T(128)S(6)} %copy.17.len_ref, bf16[4,128,128]{2,1,0:T(8,128)(2,1)} %bitcast.10, bf16[128,256]{1,0:T(8,128)(2,1)} %bitcast.11, bf16[6,2,128,256]{3,2,1,0:T(8,128)(2,1)} %pool_ref.1, bf16[512,8192]{1,0:T(8,128)(2,1)} %w_hbm.1), custom_call_target="tpu_custom_call" | custom-call | flops 3000000000 | bytes 12000000 | tf_op jit(solution)/shard_map/pallas_call | solution.py:273
  81.4 1.9 %copy.18 = bf16[1,32,8192]{2,1,0:T(8,128)(2,1)} copy(bf16[1,32,8192]{2,1,0:T(8,128)(2,1)} %bitcast.9) | data formatting | bytes 1048576
Async XLA Ops:
  0.0 0.9 %copy-start = (bf16[1,128,2,256]{3,2,1,0:T(2,128)(2,1)S(1)}, bf16[1,128,2,256]{3,2,1,0:T(2,128)(2,1)}, u32[]{:S(2)}) copy-start(bf16[1,128,2,256]{3,2,1,0:T(2,128)(2,1)} %param.8) | copy-start | bytes 393220

commit v2 on v1

--- a/solution.py
+++ b/solution.py
@@ -114,9 +114,9 @@
 
     q_own = q_ref[...].reshape(heads * rows, hd)
     scores = dot_t(q_own, suf_ref[:, :hd])
-    row = lax.broadcasted_iota(jnp.int32, (heads, rows, rows), 1).reshape(heads * rows, rows)
+    row = lax.broadcasted_iota(jnp.int32, (heads * rows, rows), 0)
     column = lax.broadcasted_iota(jnp.int32, (heads * rows, rows), 1)
-    scores = jnp.where(column <= row, scores, NEG_FILL)
+    scores = jnp.where(column * heads <= row, scores, NEG_FILL)
     att_suf, lse_suf = softmax([scores], [suf_ref[:, hd:]])
     o_suf[...] = att_suf
 
@@ -167,7 +167,10 @@
         o_copy(d).wait_recv()
         s_copy(d).wait_recv()
     stats = s_recv[...].reshape(LANES, rows).T
-    live = lax.broadcasted_iota(jnp.int32, (rows, 1), 0) < len_ref[0]
+    tokens = rows // heads
+    place = lax.broadcasted_iota(jnp.int32, (rows, 1), 0)
+    pick_to = lax.broadcasted_iota(jnp.int32, (tokens, rows), 0) * heads
+    pick_from = lax.broadcasted_iota(jnp.int32, (tokens, rows), 1)
     for j in range(heads):
         here = slice(j * rows, (j + 1) * rows)
         logs = [lse_own[here], lse_suf[here]] + [
@@ -178,7 +181,13 @@
         shares = [jnp.exp2(x - peak) for x in logs]
         total = functools.reduce(jnp.add, shares)
         mixed = functools.reduce(jnp.add, [s * o for s, o in zip(shares, parts)]) / total
-        attn[:, j * hd:(j + 1) * hd] = jnp.where(live, mixed, 0.0).astype(BF16)
+        live = place + j * rows < len_ref[0] * heads
+        mixed = jnp.where(live, mixed, 0.0).astype(BF16)
+        for h in range(heads):
+            picks = jnp.where(pick_to + h == pick_from, 1.0, 0.0).astype(BF16)
+            attn[j * tokens:(j + 1) * tokens, h * hd:(h + 1) * hd] = jnp.dot(
+                picks, mixed, preferred_element_type=F32
+            ).astype(BF16)
 
     w_copy.wait()
 
@@ -262,7 +271,7 @@
     blocks = model // block
     rows_dev = rows // tps
     group = heads * tps // kv_heads
-    q = jnp.transpose(queries[0], (1, 0, 2))
+    q = queries.reshape(heads, rows, hd)
     suffix = lax.dynamic_index_in_dim(
         suffix_kv[0], lax.axis_index("tp") * heads // group, 1, keepdims=False
     )

time: 83.5 us -> 82.1 us (0.983)
  local copies, waits for them, and re-layouts: 4.47 us -> 2.88 us
    unnamed x5 -> x4, local copies, waits for them, and re-layouts: 4.33 us -> 2.74 us
where the time goes in v2:
time: 82.1 us; the launch traced here: 81.9 us
  Pallas kernels  78.3 us (95%)
  local copies, waits for them, and re-layouts  2.88 us (4%)
    pallas_call x1, Pallas kernels, per_device(): pl.pallas_call(functools.partial(kernel, pools, tps, block), out_shape=ja...  78.3 us
    unnamed x4, local copies, waits for them, and re-layouts  2.74 us

profile of v2, /device:TPU:0, one launch (start us, length us, event | category | flops | bytes accessed | tf_op | source)
XLA Modules:
  0.0 81.9 jit_solution(13483081696450418059)
XLA Ops:
  0.0 0.0 copy-start
  0.7 0.2 copy-done
  0.9 0.1 constant_dynamic-slice_fusion
  1.1 0.6 copy.11
  1.7 78.3 %shard_map.73 = bf16[32,8192]{1,0:T(8,128)(2,1)} custom-call(s32[96]{0:T(128)} %map_ref.1, s32[4,16]{1,0:T(4,128)} %hit_ref.1, s32[1]{0:T(128)S(6)} %copy.13.len_ref, bf16[4,128,128]{2,1,0:T(8,128)(2,1)} %bitcast.7, bf16[128,256]{1,0:T(8,128)(2,1)} %bitcast.6, bf16[6,2,128,256]{3,2,1,0:T(8,128)(2,1)} %pool_ref.1, bf16[512,8192]{1,0:T(8,128)(2,1)} %w_hbm.1), custom_call_target="tpu_custom_call" | custom-call | flops 3000000000 | bytes 12000000 | tf_op jit(solution)/shard_map/pallas_call | solution.py:282
  80.0 1.9 %copy.14 = bf16[1,32,8192]{2,1,0:T(8,128)(2,1)} copy(bf16[1,32,8192]{2,1,0:T(8,128)(2,1)} %bitcast.5) | data formatting | bytes 1048576
Async XLA Ops:
  0.0 0.9 %copy-start = (bf16[1,128,2,256]{3,2,1,0:T(2,128)(2,1)S(1)}, bf16[1,128,2,256]{3,2,1,0:T(2,128)(2,1)}, u32[]{:S(2)}) copy-start(bf16[1,128,2,256]{3,2,1,0:T(2,128)(2,1)} %param.8) | copy-start | bytes 393220
